TPU v7x, 256 devices: a whole 4x4x8 slice. The times are simulated.
256 devices in a mesh: dp: 8 (over y, core), expert: 32 (over z, x).
Axes of the slice: x: 4, y: 4, z: 8, core: 2. Of those that a mesh axis runs over, the one named last changes fastest.
Arguments:
- tokens: bfloat16 [12288, 2048], P(('dp', 'expert')), may hold values from -6 to 6
- expert_ids: int32 [12288, 8], P(('dp', 'expert')), may hold values from 0 to 31, all different within a row; in each aligned block of 48 rows (0 to 47, 48 to 95, ...) at most 18 rows name the same one
- gate_weights: float32 [12288, 8], P(('dp', 'expert')), may hold values from 0.05 to 1
- up_weight: bfloat16 [32, 2048, 768], P('expert'), may hold values from -0.125 to 0.125
- down_weight: bfloat16 [32, 768, 2048], P('expert'), may hold values from -0.21875 to 0.21875
- out_grad: bfloat16 [12288, 2048], P(('dp', 'expert')), may hold values from -0.59765625 to 0.59765625
Outputs:
- mixed: bfloat16 [12288, 2048], P(('dp', 'expert'))
- grad_tokens: bfloat16 [12288, 2048], P(('dp', 'expert'))
- grad_up: bfloat16 [32, 2048, 768], P('expert')
- grad_down: bfloat16 [32, 768, 2048], P('expert')
Inputs may be any that keep to these rules, and one draw needn't show every extreme that they name: `expert_ids`: the 8 experts of a token are distinct. Among the 48 tokens of one device at most 18 name any one expert, and in every draw some device has 18 tokens naming one expert.
All inputs are finite; a program needn't handle non-finite values.
Results may differ from a plain program's by a relative error of at most 0.017.
Values may be sent and summed in bfloat16 or wider, within the bound.
A program may use at most 128 MiB of HBM per device.

v0:
```python
import jax
import jax.numpy as jnp
from jax import lax
from jax.sharding import PartitionSpec as P


def silu_slope(pre_act):
    sigmoid = jax.nn.sigmoid(pre_act)
    return sigmoid * (1.0 + pre_act * (1.0 - sigmoid))


def contract(left, right, left_dim, right_dim):
    return lax.dot_general(
        left, right, (((left_dim,), (right_dim,)), ((), ())), preferred_element_type=jnp.float32
    )


def forward_block(rows_x, up_local, down_local):
    pre_act = jnp.dot(rows_x, up_local, preferred_element_type=jnp.float32)
    hidden = jax.nn.silu(pre_act).astype(jnp.bfloat16)
    expert_out = jnp.dot(hidden, down_local, preferred_element_type=jnp.float32).astype(
        jnp.bfloat16
    )
    return (pre_act, hidden, expert_out)


def backward_block(rows_dy, pre_act, up_local, down_local):
    linear = contract(rows_dy, down_local, 1, 1)
    pre_grad = (linear * silu_slope(pre_act)).astype(jnp.bfloat16)
    grad_rows = contract(pre_grad, up_local, 1, 1).astype(jnp.bfloat16)
    return (pre_grad, grad_rows)


def shards(tokens, expert_ids, gate_weights, up_weight, down_weight, out_grad):
    experts = lax.axis_size("expert")
    tok_count, top_count = expert_ids.shape
    slot_rows = tok_count * top_count * 3 // (2 * experts)
    recv_rows = experts * slot_rows
    model_width = tokens.shape[1]
    up_local = up_weight[0]
    down_local = down_weight[0]
    matches = (
        expert_ids[:, :, None] == jnp.arange(experts, dtype=jnp.int32)[None, None, :]
    ).astype(jnp.int32)
    hit_table = jnp.sum(matches, axis=1)
    before = jnp.cumsum(hit_table, axis=0) - hit_table
    slot_place = jnp.sum(matches * before[:, None, :], axis=2)
    target = (expert_ids * slot_rows + slot_place).reshape(-1)
    source = jnp.repeat(
        jnp.arange(tok_count, dtype=jnp.int32), top_count, total_repeat_length=tok_count * top_count
    )
    counts = jnp.sum(hit_table, axis=0).astype(jnp.bfloat16).reshape(experts, 1)
    send_x = jnp.zeros((recv_rows, model_width), jnp.bfloat16).at[target].set(tokens[source])
    send_x = send_x.reshape(experts, slot_rows, model_width)
    scaled = (gate_weights.reshape(-1)[:, None] * out_grad[source].astype(jnp.float32)).astype(
        jnp.bfloat16
    )
    send_dy = jnp.zeros((recv_rows, model_width), jnp.bfloat16).at[target].set(scaled)
    send_dy = send_dy.reshape(experts, slot_rows, model_width)
    got_x, got_counts = (
        lax.all_to_all(send_x, "expert", split_axis=0, concat_axis=0, tiled=True),
        lax.all_to_all(counts, "expert", split_axis=0, concat_axis=0, tiled=True),
    )
    x_rows = got_x.reshape(recv_rows, model_width)
    pre_rows, hidden_rows, out_rows = forward_block(x_rows, up_local, down_local)
    back_out = lax.all_to_all(
        out_rows.reshape(experts, slot_rows, model_width),
        "expert",
        split_axis=0,
        concat_axis=0,
        tiled=True,
    )
    gathered = back_out.reshape(recv_rows, model_width)[target].reshape(
        tok_count, top_count, model_width
    )
    mixed = jnp.sum(gate_weights[:, :, None] * gathered.astype(jnp.float32), axis=1).astype(
        jnp.bfloat16
    )
    got_dy = lax.all_to_all(send_dy, "expert", split_axis=0, concat_axis=0, tiled=True)
    dy_rows = got_dy.reshape(recv_rows, model_width)
    down_grad = contract(hidden_rows, dy_rows, 0, 0)
    pre_grad, grad_rows = backward_block(dy_rows, pre_rows, up_local, down_local)
    up_grad = contract(x_rows, pre_grad, 0, 0)
    back_grad = lax.all_to_all(
        grad_rows.reshape(experts, slot_rows, model_width),
        "expert",
        split_axis=0,
        concat_axis=0,
        tiled=True,
    )
    grad_pairs = back_grad.reshape(recv_rows, model_width)[target].reshape(
        tok_count, top_count, model_width
    )
    grad_tokens = jnp.sum(grad_pairs.astype(jnp.float32), axis=1).astype(jnp.bfloat16)
    up_sum, down_sum = (
        lax.psum(up_grad.astype(jnp.bfloat16), "dp").astype(jnp.float32),
        lax.psum(down_grad.astype(jnp.bfloat16), "dp").astype(jnp.float32),
    )
    return (
        mixed,
        grad_tokens,
        up_sum.astype(jnp.bfloat16)[None],
        down_sum.astype(jnp.bfloat16)[None],
    )


def solution(mesh):
    return jax.shard_map(
        shards,
        mesh=mesh,
        in_specs=(
            P(("dp", "expert"), None),
            P(("dp", "expert"), None),
            P(("dp", "expert"), None),
            P("expert", None, None),
            P("expert", None, None),
            P(("dp", "expert"), None),
        ),
        out_specs=(
            P(("dp", "expert"), None),
            P(("dp", "expert"), None),
            P("expert", None, None),
            P("expert", None, None),
        ),
        check_vma=False,
    )
```

profile of v0, /device:TPU:1, one launch (start us, length us, event | category | flops | bytes accessed | tf_op | source)
XLA Modules:
  0.0 419.1 jit_solution(2827004243275815858)
XLA Ops:
  7.2 0.7 fusion.33
  7.9 0.7 fusion.31
  8.6 0.7 fusion.32
  9.3 0.7 convert_reduce_fusion
  10.1 0.8 fusion.25
  10.9 4.5 %fusion.27 = (s32[384]{0:T(512)S(1)}, s32[384,1]{0,1:T(1,128)S(1)}) fusion(s32[]{:T(128)} %bitcast.41, s32[]{:T(128)} %bitcast.42, s32[]{:T(128)} %bitcast.43, s32[]{:T(128)} %bitcast.44, s32[]{:T(128)} %bitcast.45, s32[]{:T(128)} %bitcast.47, s32[]{:T(128)} %bitcast.46, s32[1,1,3,128]{3,2,1,0:T(4,128)S(1)} %get-tuple-element.62, ...), kind=kLoop, calls=%fused_computation.95 | loop fusion | flops 5376 | bytes 6172 | tf_op jit(solution)/shard_map/jit(_take)/gather | solution.py:49
  15.4 0.2 compare_reduce_fusion.40
  15.6 25.6 %select_select_fusion = s32[384]{0:T(512)S(1)} fusion(pred[384]{0:T(512)(128)(4,1)S(1)} %get-tuple-element.55, pred[384]{0:T(512)(128)(4,1)S(1)} %get-tuple-element.54, pred[384]{0:T(512)(128)(4,1)S(1)} %get-tuple-element.56, pred[384]{0:T(512)(128)(4,1)S(1)} %get-tuple-element.53, pred[384]{0:T(512)(128)(4,1)S(1)} %get-tuple-element.52, ...), kind=kLoop, calls=%fused_computation.94 | loop fusion | flops 15744 | bytes 18980 | tf_op jit(solution)/shard_map/jit(_take)/gather | solution.py:49
  41.4 0.7 select_reduce_fusion
  42.1 0.7 multiply_add_fusion
  42.8 0.1 copy.20
  42.9 0.1 reshape.185
  43.0 10.9 %scatter_custom_fusion = bf16[576,2048]{1,0:T(8,128)(2,1)} fusion(s32[384]{0:T(512)S(1)} %fusion.28, bf16[48,2048]{1,0:T(8,128)(2,1)} %param.8, s32[1024]{0:T(1024)S(1)} %pad_clamp_fusion.1, bf16[]{:T(256)} %constant.95.clone.1), kind=kCustom, calls=%fused_computation.28 | custom fusion | bytes 2359808 | tf_op jit(solution)/shard_map/scatter | solution.py:53
  53.9 4.3 %reshape.186 = bf16[32,18,2048]{2,1,0:T(8,128)(2,1)} reshape(bf16[576,2048]{1,0:T(8,128)(2,1)} %scatter_custom_fusion) | data formatting | bytes 4718592 | tf_op jit(solution)/shard_map/reshape | solution.py:54
  58.2 12.3 %all-to-all-start = ((bf16[32,18,2048]{2,1,0:T(8,128)(2,1)}), bf16[32,18,2048]{2,1,0:T(8,128)(2,1)}, u32[]{:S(2)}, u32[]{:S(2)}) async-start(bf16[32,18,2048]{2,1,0:T(8,128)(2,1)} %reshape.186), calls=%async_computation | async-start | bytes 6291456 | tf_op jit(solution)/shard_map/all_to_all | solution.py:61
  70.5 0.1 copy.16
  70.6 0.1 mul.52
  70.7 9.6 %scatter_custom_fusion.1 = bf16[576,2048]{1,0:T(8,128)(2,1)} fusion(s32[384]{0:T(512)S(1)} %fusion.28, f32[384]{0:T(512)S(1)} %mul.52, bf16[]{:T(256)} %constant.95.clone.1, bf16[48,2048]{1,0:T(8,128)(2,1)S(1)} %copy-done.6, s32[1024]{0:T(1024)S(1)} %pad_clamp_fusion.1), kind=kCustom, calls=%fused_computation.26 | custom fusion | flops 2359296 | bytes 2562050 | tf_op jit(solution)/shard_map/scatter | solution.py:58
  80.3 4.3 %reshape.190 = bf16[32,18,2048]{2,1,0:T(8,128)(2,1)} reshape(bf16[576,2048]{1,0:T(8,128)(2,1)} %scatter_custom_fusion.1) | data formatting | bytes 4718592 | tf_op jit(solution)/shard_map/reshape | solution.py:59
  84.6 56.4 %all-to-all-done = bf16[32,18,2048]{2,1,0:T(8,128)(2,1)} async-done(((bf16[32,18,2048]{2,1,0:T(8,128)(2,1)}), bf16[32,18,2048]{2,1,0:T(8,128)(2,1)}, u32[]{:S(2)}, u32[]{:S(2)}) %all-to-all-start) | async-done | bytes 2359328 | tf_op jit(solution)/shard_map/all_to_all | solution.py:61
  141.0 7.9 %all-to-all-start.2 = ((bf16[32,18,2048]{2,1,0:T(8,128)(2,1)}), bf16[32,18,2048]{2,1,0:T(8,128)(2,1)}, u32[]{:S(2)}, u32[]{:S(2)}) async-start(bf16[32,18,2048]{2,1,0:T(8,128)(2,1)} %reshape.190), calls=%async_computation.2 | async-start | bytes 6291456 | tf_op jit(solution)/shard_map/all_to_all | solution.py:79
  148.9 4.4 %reshape.187 = bf16[576,2048]{1,0:T(8,128)(2,1)} reshape(bf16[32,18,2048]{2,1,0:T(8,128)(2,1)} %all-to-all-done) | data formatting | bytes 4718592 | tf_op jit(solution)/shard_map/reshape | solution.py:64
  153.3 4.6 %fusion.7 = f32[576,768]{1,0:T(8,128)S(1)} fusion(bf16[576,2048]{1,0:T(8,128)(2,1)} %reshape.187, bf16[1,2048,768]{2,1,0:T(8,128)(2,1)} %param.11), kind=kOutput, calls=%fused_computation.16 | convolution fusion | flops 1811939328 | bytes 7274496 | tf_op jit(solution)/shard_map/dot_general | solution.py:19
  157.9 1.2 copy-done.9
  159.1 3.5 fusion.12
  162.5 4.3 %reshape.188 = bf16[32,18,2048]{2,1,0:T(8,128)(2,1)} reshape(bf16[576,2048]{1,0:T(8,128)(2,1)} %fusion.12) | data formatting | bytes 4718592 | tf_op jit(solution)/shard_map/reshape | solution.py:67
  166.8 52.9 %all-to-all-done.2 = bf16[32,18,2048]{2,1,0:T(8,128)(2,1)} async-done(((bf16[32,18,2048]{2,1,0:T(8,128)(2,1)}), bf16[32,18,2048]{2,1,0:T(8,128)(2,1)}, u32[]{:S(2)}, u32[]{:S(2)}) %all-to-all-start.2) | async-done | bytes 2359328 | tf_op jit(solution)/shard_map/all_to_all | solution.py:79
  219.7 6.6 %all-to-all-start.1 = ((bf16[32,18,2048]{2,1,0:T(8,128)(2,1)}), bf16[32,18,2048]{2,1,0:T(8,128)(2,1)}, u32[]{:S(2)}, u32[]{:S(2)}) async-start(bf16[32,18,2048]{2,1,0:T(8,128)(2,1)} %reshape.188), calls=%async_computation.1 | async-start | bytes 6291456 | tf_op jit(solution)/shard_map/all_to_all | solution.py:66
  226.4 4.4 %reshape.191 = bf16[576,2048]{1,0:T(8,128)(2,1)} reshape(bf16[32,18,2048]{2,1,0:T(8,128)(2,1)} %all-to-all-done.2) | data formatting | bytes 4718592 | tf_op jit(solution)/shard_map/reshape | solution.py:80
  230.8 4.6 %multiply_convert_fusion.1 = bf16[576,768]{1,0:T(8,128)(2,1)S(1)} fusion(f32[576,768]{1,0:T(8,128)} %copy-done.9, bf16[576,2048]{1,0:T(8,128)(2,1)} %reshape.191, bf16[1,768,2048]{2,1,0:T(8,128)(2,1)S(1)} %copy-done), kind=kOutput, calls=%fused_computation.23 | convolution fusion | flops 1815920640 | bytes 8159232 | tf_op jit(solution)/shard_map/dot_general | solution.py:13
  235.4 1.0 copy-done.11
  236.4 2.0 fusion.9
  238.4 2.4 reshape.192
  240.8 55.6 %all-to-all-done.1 = bf16[32,18,2048]{2,1,0:T(8,128)(2,1)} async-done(((bf16[32,18,2048]{2,1,0:T(8,128)(2,1)}), bf16[32,18,2048]{2,1,0:T(8,128)(2,1)}, u32[]{:S(2)}, u32[]{:S(2)}) %all-to-all-start.1) | async-done | bytes 2359328 | tf_op jit(solution)/shard_map/all_to_all | solution.py:66
  296.4 6.8 %all-to-all-start.3 = ((bf16[32,18,2048]{2,1,0:T(8,128)(2,1)}), bf16[32,18,2048]{2,1,0:T(8,128)(2,1)}, u32[]{:S(2)}, u32[]{:S(2)}) async-start(bf16[32,18,2048]{2,1,0:T(8,128)(2,1)} %reshape.192), calls=%async_computation.3 | async-start | bytes 6291456 | tf_op jit(solution)/shard_map/all_to_all | solution.py:84
  303.2 0.3 all-reduce.3.cloned.1.call-start
  303.5 5.4 %fusion.15 = bf16[1,2048,768]{2,1,0:T(8,128)(2,1)} fusion(bf16[576,2048]{1,0:T(8,128)(2,1)S(1)} %copy-done.4, bf16[576,768]{1,0:T(8,128)(2,1)} %copy-done.11), kind=kOutput, calls=%fused_computation.21 | convolution fusion | flops 1813512192 | bytes 6389760 | tf_op jit(solution)/shard_map/dot_general | solution.py:13
  308.9 4.1 fusion.16
  313.0 2.9 reshape.189
  316.0 3.1 gather_fusion
  319.1 53.4 %all-to-all-done.3 = bf16[32,18,2048]{2,1,0:T(8,128)(2,1)} async-done(((bf16[32,18,2048]{2,1,0:T(8,128)(2,1)}), bf16[32,18,2048]{2,1,0:T(8,128)(2,1)}, u32[]{:S(2)}, u32[]{:S(2)}) %all-to-all-start.3) | async-done | bytes 2359328 | tf_op jit(solution)/shard_map/all_to_all | solution.py:84
  372.5 3.1 reshape.193
  375.6 3.1 gather_fusion.1
  378.7 3.3 bitcast_reduce_fusion
  382.0 2.1 fusion
  384.1 22.6 %all-reduce.3.cloned.1.call-done = (bf16[1,2048,768]{2,1,0:T(8,128)(2,1)}, bf16[1,768,2048]{2,1,0:T(8,128)(2,1)}) async-done(((bf16[1,2048,768]{2,1,0:T(8,128)(2,1)}, bf16[1,768,2048]{2,1,0:T(8,128)(2,1)}), (bf16[1,2048,768]{2,1,0:T(8,128)(2,1)}, bf16[1,768,2048]{2,1,0:T(8,128)(2,1)})) %all-reduce.3.cloned.1.call-update) | async-done | bytes 6291472 | tf_op jit(solution)/shard_map/psum | solution.py:96
  406.7 3.9 copy.30
  410.6 1.7 copy.31
  (33 shorter events, 0.4 us)
Async XLA Ops:
  7.2 151.9 %copy-start = (bf16[1,768,2048]{2,1,0:T(8,128)(2,1)S(1)}, bf16[1,768,2048]{2,1,0:T(8,128)(2,1)}, u32[]{:S(2)}) copy-start(bf16[1,768,2048]{2,1,0:T(8,128)(2,1)} %param.12) | copy-start | bytes 9437188
  58.2 12.3 %copy-start.7 = (f32[48,8]{0,1:T(8,128)S(1)}, f32[48,8]{0,1:T(8,128)}, u32[]{:S(2)}) copy-start(f32[48,8]{0,1:T(8,128)} %param.10) | copy-start | bytes 4612
  58.2 12.5 %copy-start.6 = (bf16[48,2048]{1,0:T(8,128)(2,1)S(1)}, bf16[48,2048]{1,0:T(8,128)(2,1)}, u32[]{:S(2)}) copy-start(bf16[48,2048]{1,0:T(8,128)(2,1)} %param.13) | copy-start | bytes 589828
  58.2 82.8 %all-to-all-start = ((bf16[32,18,2048]{2,1,0:T(8,128)(2,1)}), bf16[32,18,2048]{2,1,0:T(8,128)(2,1)}, u32[]{:S(2)}, u32[]{:S(2)}) async-start(bf16[32,18,2048]{2,1,0:T(8,128)(2,1)} %reshape.186), calls=%async_computation | async-start | bytes 6291456 | tf_op jit(solution)/shard_map/all_to_all | solution.py:61
  141.0 78.7 %all-to-all-start.2 = ((bf16[32,18,2048]{2,1,0:T(8,128)(2,1)}), bf16[32,18,2048]{2,1,0:T(8,128)(2,1)}, u32[]{:S(2)}, u32[]{:S(2)}) async-start(bf16[32,18,2048]{2,1,0:T(8,128)(2,1)} %reshape.190), calls=%async_computation.2 | async-start | bytes 6291456 | tf_op jit(solution)/shard_map/all_to_all | solution.py:79
  157.9 1.2 copy-start.9
  219.7 76.7 %all-to-all-start.1 = ((bf16[32,18,2048]{2,1,0:T(8,128)(2,1)}), bf16[32,18,2048]{2,1,0:T(8,128)(2,1)}, u32[]{:S(2)}, u32[]{:S(2)}) async-start(bf16[32,18,2048]{2,1,0:T(8,128)(2,1)} %reshape.188), calls=%async_computation.1 | async-start | bytes 6291456 | tf_op jit(solution)/shard_map/all_to_all | solution.py:66
  230.8 5.6 %copy-start.8 = (bf16[1,2048,768]{2,1,0:T(8,128)(2,1)S(1)}, bf16[1,2048,768]{2,1,0:T(8,128)(2,1)}, u32[]{:S(2)}) copy-start(bf16[1,2048,768]{2,1,0:T(8,128)(2,1)} %param.11) | copy-start | bytes 9437188
  235.4 1.0 copy-start.11
  240.8 62.7 %copy-start.4 = (bf16[576,2048]{1,0:T(8,128)(2,1)S(1)}, bf16[576,2048]{1,0:T(8,128)(2,1)}, u32[]{:S(2)}) copy-start(bf16[576,2048]{1,0:T(8,128)(2,1)} %reshape.187) | copy-start | bytes 7077892
  296.4 76.1 %all-to-all-start.3 = ((bf16[32,18,2048]{2,1,0:T(8,128)(2,1)}), bf16[32,18,2048]{2,1,0:T(8,128)(2,1)}, u32[]{:S(2)}, u32[]{:S(2)}) async-start(bf16[32,18,2048]{2,1,0:T(8,128)(2,1)} %reshape.192), calls=%async_computation.3 | async-start | bytes 6291456 | tf_op jit(solution)/shard_map/all_to_all | solution.py:84
  303.2 103.5 %all-reduce.3.cloned.1.call-start = ((), (), s32[]{:S(2)}) async-start(), calls=%async_computation.4 | async-start | bytes 12582912 | tf_op jit(solution)/shard_map/psum | solution.py:96
  303.5 5.4 %copy-start.5 = (bf16[576,2048]{1,0:T(8,128)(2,1)S(1)}, bf16[576,2048]{1,0:T(8,128)(2,1)}, u32[]{:S(2)}) copy-start(bf16[576,2048]{1,0:T(8,128)(2,1)} %reshape.191) | copy-start | bytes 7077892
  303.5 5.4 %copy-start.10 = (f32[576,768]{1,0:T(8,128)S(1)}, f32[576,768]{1,0:T(8,128)}, u32[]{:S(2)}) copy-start(f32[576,768]{1,0:T(8,128)} %copy-done.9) | copy-start | bytes 5308420
  378.7 3.3 copy-start.2
  406.7 3.9 copy-start.3
  406.7 5.6 %copy-start.1 = (bf16[1,768,2048]{2,1,0:T(8,128)(2,1)S(1)}, bf16[1,768,2048]{2,1,0:T(8,128)(2,1)}, u32[]{:S(2)}) copy-start(bf16[1,768,2048]{2,1,0:T(8,128)(2,1)} %param.12) | copy-start | bytes 9437188
Sparse Core Ops, SparseCore 0:
  313.1 93.5 all-reduce.2
where the time goes:
time: 421 us; the launch traced here: 419 us
  waiting for transfers between devices  241 us (57%)
  local copies, waits for them, and re-layouts  57.6 us (14%)
  other arithmetic  48.4 us (11%)
  starting transfers between devices  33.9 us (8%)
  matrix products  24.1 us (6%)
  between operations  14.2 us (3%)
    all_to_all x1, waiting for transfers between devices, shards(): lax.all_to_all(send_x, 'expert', split_axis=0, concat_axis=0, tiled=True)  56.4 us
    all_to_all x1, waiting for transfers between devices, shards(): lax.all_to_all(out_rows.reshape(experts, slot_rows, model_width), 'expert...  55.6 us
    all_to_all x1, waiting for transfers between devices, shards(): lax.all_to_all(grad_rows.reshape(experts, slot_rows, model_width), 'exper...  53.4 us
    all_to_all x1, waiting for transfers between devices, shards(): lax.all_to_all(send_dy, 'expert', split_axis=0, concat_axis=0, tiled=True)  52.9 us
    gather x3, other arithmetic, shards(): jnp.repeat(jnp.arange(tok_count, dtype=jnp.int32), top_count, total_repea...  30.3 us
    psum x1, waiting for transfers between devices, shards(): lax.psum(up_grad.astype(jnp.bfloat16), 'dp').astype(jnp.float32)  22.6 us
    dot_general x4, matrix products, contract(): lax.dot_general(left, right, (((left_dim,), (right_dim,)), ((), ())), pre...  16.1 us
    all_to_all x1, starting transfers between devices, shards(): lax.all_to_all(send_x, 'expert', split_axis=0, concat_axis=0, tiled=True)  12.3 us
  transfers between devices with their start and end apart: 5, of which 5 were waited for; matrix products, arithmetic and copies ran while one was open for 17% of the time, Pallas kernels for 0%

commit v1 on v0

v1 whole, which is shorter than its diff:
```python
import functools

import jax
import jax.numpy as jnp
from jax import lax
from jax.experimental import pallas as pl
from jax.experimental.pallas import tpu as pltpu
from jax.sharding import PartitionSpec as P

BF16 = jnp.bfloat16
F32 = jnp.float32
MESH_ID = pl.DeviceIdType.MESH


def mm(left, right, left_dim=1, right_dim=0):
    return lax.dot_general(
        left, right, (((left_dim,), (right_dim,)), ((), ())), preferred_element_type=F32
    )


class Cfg:
    def __init__(self, nz, nx, ny, tok, top, width, hidden, nc):
        self.nz, self.nx, self.ny = nz, nx, ny
        self.tok, self.top, self.width, self.hidden, self.nc = tok, top, width, hidden, nc
        self.experts = nz * nx
        self.slot = tok * top * 3 // (2 * self.experts)
        self.rows_x = nz * self.slot
        self.rows = nx * self.rows_x
        self.seen = nz * tok
        self.cw = width // nc


def kernel(cfg, *refs):
    nz, nx, ny, tok, nc, cw = cfg.nz, cfg.nx, cfg.ny, cfg.tok, cfg.nc, cfg.cw
    rx, rows, seen, experts = cfg.rows_x, cfg.rows, cfg.seen, cfg.experts
    width, hid_w = cfg.width, cfg.hidden
    (tok_ref, og_ref, ids_ref, gate_ref, up_hbm, down_hbm, mixed_ref, gtok_ref, gup_ref, gdown_ref) = refs[:10]
    (zbuf, zmeta, xsend, xrecv, upv, downv, pre, lin, hid, pgr, onehot, onehot_t, gates,
     csend, crecv, pbuf, rsbuf, fin, g_down, g_up, c_down, c_up, r_down, r_up, f_down, f_up,
     w_sem, z_ss, z_rs, x_ss, x_rs, c_ss, c_rs, s_ss, s_rs, y_ss, y_rs, l_sem) = refs[10:]

    dp = lax.axis_index("dp")
    ex = lax.axis_index("expert")
    y, core = dp // 2, lax.rem(dp, 2)
    z, x = ex // nx, lax.rem(ex, nx)

    def at_z(step):
        return (dp, lax.rem(z + step + nz, nz) * nx + x)

    def at_x(step):
        return (dp, z * nx + lax.rem(x + step + nx, nx))

    def at_y(step):
        return (lax.rem(y + step + ny, ny) * 2 + core, ex)

    other_core = (y * 2 + 1 - core, ex)

    def copy(src, dst, ss, rs, to):
        return pltpu.make_async_remote_copy(
            src_ref=src, dst_ref=dst, send_sem=ss, recv_sem=rs, device_id=to, device_id_type=MESH_ID
        )

    w_up = pltpu.make_async_copy(up_hbm.at[0], upv, w_sem.at[0])
    w_down = pltpu.make_async_copy(down_hbm.at[0], downv, w_sem.at[1])
    w_up.start()
    w_down.start()

    partners = [at_z(1), at_z(-1)] + [at_x(j) for j in range(1, nx)]
    if ny > 1:
        partners += [at_y(1), at_y(-1), other_core]
    barrier = pltpu.get_barrier_semaphore()
    for partner in partners:
        pl.semaphore_signal(barrier, inc=1, device_id=partner, device_id_type=MESH_ID)

    for k in range(nc):
        zbuf[k, 0:tok, :] = tok_ref[:, k * cw:(k + 1) * cw]
        zbuf[nc + k, 0:tok, :] = og_ref[:, k * cw:(k + 1) * cw]
    lane = lax.broadcasted_iota(jnp.int32, (tok, 128), 1)
    lane_e = lane & (experts - 1)
    hit = jnp.zeros((tok, 128), F32)
    gate = jnp.zeros((tok, 128), F32)
    for k in range(cfg.top):
        match = ids_ref[:, k:k + 1] == lane_e
        hit = hit + jnp.where(match, 1.0, 0.0)
        gate = gate + jnp.where(match, gate_ref[:, k:k + 1], 0.0)
    row_t = lax.broadcasted_iota(jnp.int32, (tok, tok), 0)
    col_t = lax.broadcasted_iota(jnp.int32, (tok, tok), 1)
    earlier = jnp.where(col_t < row_t, 1.0, 0.0).astype(BF16)
    before = mm(earlier, hit.astype(BF16))
    place = jnp.where(hit > 0.5, before, -1.0)
    high = gate.astype(BF16).astype(F32)
    rest = gate - high
    middle = rest.astype(BF16).astype(F32)
    low = rest - middle
    table = jnp.where(
        lane < experts, place,
        jnp.where(lane < 2 * experts, high,
                  jnp.where(lane < 3 * experts, middle,
                            jnp.where(lane < 4 * experts, low, 0.0))))
    zmeta[0:tok, :] = table.astype(BF16)

    pl.semaphore_wait(barrier, len(partners))

    def ways(k):
        plus = nz // 2 if k % 2 == 0 else (nz - 1) // 2
        return plus, nz - 1 - plus

    def z_copy(k, way, hop):
        source = hop - 1 if way == 0 else (nz - hop + 1) % nz
        target = hop if way == 0 else nz - hop
        buf = zmeta if k == 2 * nc else zbuf.at[k]
        return copy(
            buf.at[pl.ds(source * tok, tok)], buf.at[pl.ds(target * tok, tok)],
            z_ss.at[k, target - 1], z_rs.at[k, target - 1], at_z(1 if way == 0 else -1))

    def z_step(k, hop):
        for way in (0, 1):
            if 1 <= hop <= ways(k)[way]:
                z_copy(k, way, hop).wait_recv()
            if hop + 1 <= ways(k)[way]:
                z_copy(k, way, hop + 1).start()

    def build_tables():
        meta = zmeta[...].astype(F32)
        lanes = lax.broadcasted_iota(jnp.int32, (seen, 128), 1)
        row = lax.broadcasted_iota(jnp.int32, (seen, 1), 0)
        source = jnp.zeros((seen, 1), F32)
        for q in range(1, nz):
            source = source + jnp.where(row >= q * tok, 1.0, 0.0)
        wide = -(-rows // 128) * 128
        place_lane = lax.broadcasted_iota(jnp.int32, (seen, wide), 1)
        hot = jnp.zeros((seen, wide), F32)
        for j in range(nx):
            expert = z * nx + lax.rem(x + j, nx)
            spot = jnp.sum(jnp.where(lanes == expert, meta, 0.0), axis=1, keepdims=True)
            value = jnp.where(spot > -0.5, spot + cfg.slot * source + rx * j, -1.0).astype(jnp.int32)
            hot = hot + jnp.where(place_lane == value, 1.0, 0.0)
        onehot_t[...] = hot[:, 0:rows].astype(BF16)
        onehot[...] = hot.T[0:rows].astype(BF16)
        picked = mm(onehot[...], zmeta[...])
        lanes_r = lax.broadcasted_iota(jnp.int32, (rx, 128), 1)
        for j in range(nx):
            expert = z * nx + lax.rem(x + j, nx)
            mine = ((lanes_r & (experts - 1)) == expert) & (lanes_r >= experts)
            value = jnp.sum(jnp.where(mine, picked[j * rx:(j + 1) * rx], 0.0), axis=1, keepdims=True)
            gates[j * rx:(j + 1) * rx, :] = jnp.broadcast_to(value, (rx, 128))

    def x_copy(k, j):
        return copy(
            xsend.at[k, pl.ds((j - 1) * rx, rx)], xrecv.at[k, pl.ds(j * rx, rx)],
            x_ss.at[k, j - 1], x_rs.at[k, j - 1], at_x(j))

    def dispatch(k):
        packed = mm(onehot[...], zbuf[k])
        if k >= nc:
            packed = packed * gates[:, 0:1]
        packed = packed.astype(BF16)
        xsend[k] = packed[rx:]
        xrecv[k, 0:rx, :] = packed[0:rx]
        for j in range(1, nx):
            x_copy(k, j).start()

    def arrive(k):
        for j in range(1, nx):
            x_copy(k, j).wait_recv()
        if k < nc:
            if k == 0:
                w_up.wait()
            part = mm(xrecv[k], upv[k * cw:(k + 1) * cw, :])
            if k == 0:
                pre[...] = part
            else:
                pre[...] += part
        else:
            c = k - nc
            if c == 0:
                w_down.wait()
            part = mm(xrecv[k], downv[:, c * cw:(c + 1) * cw], 1, 1)
            if c == 0:
                lin[...] = part
            else:
                lin[...] += part
            g_down[:, c * cw:(c + 1) * cw] = mm(hid[...], xrecv[k], 0, 0).astype(BF16)

    blk = 16

    def make_hidden():
        def body(i, carry):
            at = pl.ds(pl.multiple_of(i * blk, blk), blk)
            p = pre[at, :]
            hid[at, :] = (p * jax.nn.sigmoid(p)).astype(BF16)
            return carry
        lax.fori_loop(0, rows // blk, body, 0)

    def make_pre_grad():
        def body(i, carry):
            at = pl.ds(pl.multiple_of(i * blk, blk), blk)
            p = pre[at, :]
            s = jax.nn.sigmoid(p)
            pgr[at, :] = (lin[at, :] * (s * (1.0 + p * (1.0 - s)))).astype(BF16)
            return carry
        lax.fori_loop(0, rows // blk, body, 0)

    def c_copy(m, j):
        return copy(
            csend.at[m, pl.ds((j - 1) * rx, rx)], crecv.at[m, pl.ds(j * rx, rx)],
            c_ss.at[m, j - 1], c_rs.at[m, j - 1], at_x(-j))

    def send_back(m):
        c = m % nc
        if m < nc:
            out = mm(hid[...], downv[:, c * cw:(c + 1) * cw])
        else:
            out = mm(pgr[...], upv[c * cw:(c + 1) * cw, :], 1, 1)
        out = out.astype(BF16)
        csend[m] = out[rx:]
        crecv[m, 0:rx, :] = out[0:rx]
        for j in range(1, nx):
            c_copy(m, j).start()

    def s_copy(m, way, hop):
        plus, minus = ways(m)
        slot = plus - hop + 1 if way == 0 else nz - (minus - hop + 1)
        at = hop - 1 if way == 0 else plus + hop - 1
        return copy(
            pbuf.at[m, pl.ds(slot * tok, tok)], rsbuf.at[m, at],
            s_ss.at[m, at], s_rs.at[m, at], at_z(-1 if way == 0 else 1))

    def s_step(m, hop):
        for way in (0, 1):
            count = ways(m)[way]
            if 1 <= hop <= count:
                s_copy(m, way, hop).wait_recv()
                at = hop - 1 if way == 0 else ways(m)[0] + hop - 1
                got = rsbuf[m, at].astype(F32)
                left = count - hop
                if left == 0:
                    fin[m] += got
                else:
                    slot = left if way == 0 else nz - left
                    sl = slice(slot * tok, (slot + 1) * tok)
                    pbuf[m, sl, :] = (pbuf[m, sl, :].astype(F32) + got).astype(BF16)
            if hop + 1 <= count:
                s_copy(m, way, hop + 1).start()
        if hop == max(ways(m)):
            c = m % nc
            target = mixed_ref if m < nc else gtok_ref
            target[:, c * cw:(c + 1) * cw] = fin[m].astype(BF16)

    def combine(m):
        for j in range(1, nx):
            c_copy(m, j).wait_recv()
        got = crecv[m]
        if m < nc:
            got = (got.astype(F32) * gates[:, 0:1]).astype(BF16)
        part = mm(onehot_t[...], got)
        fin[m] = part[0:tok]
        pbuf[m, tok:, :] = part[tok:].astype(BF16)
        s_step(m, 0)

    mats = [(g_down, c_down, r_down, f_down, gdown_ref), (g_up, c_up, r_up, f_up, gup_ref)]

    def y_copies(w):
        g, cr, r, f, out = mats[w]
        half = g.shape[0] // 2
        shard = half // 4
        part = shard // 2

        def of(step, b=0):
            return pl.multiple_of(lax.rem(y + step + ny, ny) * shard + b * part, part)

        def final(step, b, count):
            return out.at[0, pl.ds(pl.multiple_of(core * half + of(step, b), part), count)]

        def sem(i):
            return y_ss.at[w, i], y_rs.at[w, i]

        return dict(
            core=lambda: copy(g.at[pl.ds(pl.multiple_of((1 - core) * half, half), half)], cr, *sem(0), other_core),
            far_a=lambda: copy(cr.at[pl.ds(of(2, 0), part)], r.at[0], *sem(1), at_y(1)),
            far_b=lambda: copy(cr.at[pl.ds(of(2, 1), part)], r.at[1], *sem(2), at_y(-1)),
            near_b=lambda: copy(cr.at[pl.ds(of(1, 1), part)], r.at[2], *sem(3), at_y(1)),
            near_a=lambda: copy(cr.at[pl.ds(of(-1, 0), part)], r.at[3], *sem(4), at_y(-1)),
            two_a=lambda: copy(r.at[0], r.at[4], *sem(5), at_y(1)),
            two_b=lambda: copy(r.at[1], r.at[5], *sem(6), at_y(-1)),
            out_p=lambda: copy(f, final(0, 0, shard), *sem(7), at_y(1)),
            out_m=lambda: copy(f, final(0, 0, shard), *sem(8), at_y(-1)),
            out_c=lambda: copy(f, final(0, 0, shard), *sem(9), other_core),
            fwd_a=lambda: copy(final(-1, 0, part), final(-1, 0, part), *sem(10), at_y(1)),
            fwd_b=lambda: copy(final(1, 1, part), final(1, 1, part), *sem(11), at_y(-1)),
            cor_p=lambda: copy(final(-1, 0, shard), final(-1, 0, shard), *sem(12), other_core),
            cor_m=lambda: copy(final(1, 0, shard), final(1, 0, shard), *sem(13), other_core),
            cor_f=lambda: copy(final(2, 0, shard), final(2, 0, shard), *sem(14), other_core),
            own=lambda: pltpu.make_async_copy(f, final(0, 0, shard), l_sem.at[w]),
        )

    def add_rows(target, t0, source, s0, count, extra=None):
        size = 16 if count % 16 == 0 else count

        def body(i, carry):
            a = pl.ds(pl.multiple_of(t0 + i * size, size), size)
            b = pl.ds(pl.multiple_of(s0 + i * size, size), size)
            target[a, :] = (target[a, :].astype(F32) + source[b, :].astype(F32)).astype(BF16)
            return carry
        lax.fori_loop(0, count // size, body, 0)

    def y_step(w, step):
        g, cr, r, f, out = mats[w]
        half = g.shape[0] // 2
        shard = half // 4
        part = shard // 2
        cp = y_copies(w)

        def of(move, b=0):
            return pl.multiple_of(lax.rem(y + move + ny, ny) * shard + b * part, part)

        if step == 1:
            cp["core"]().start()
        elif step == 2:
            cp["core"]().wait_recv()
            add_rows(cr, 0, g, pl.multiple_of(core * half, half), half)
            for name in ("far_a", "far_b", "near_b", "near_a"):
                cp[name]().start()
        elif step == 3:
            cp["far_a"]().wait_recv()
            add_rows(r.at[0], 0, cr, of(1, 0), part)
            cp["two_a"]().start()
            cp["far_b"]().wait_recv()
            add_rows(r.at[1], 0, cr, of(-1, 1), part)
            cp["two_b"]().start()
        elif step == 4:
            for name in ("near_a", "near_b", "two_a", "two_b"):
                cp[name]().wait_recv()
            size = 16 if part % 16 == 0 else part
            for b, near, two in ((0, 3, 4), (1, 2, 5)):
                def body(i, carry):
                    a = pl.ds(pl.multiple_of(i * size, size), size)
                    c = pl.ds(pl.multiple_of(of(0, b) + i * size, size), size)
                    total = cr[c, :].astype(F32) + r[near, a, :].astype(F32) + r[two, a, :].astype(F32)
                    f[pl.ds(pl.multiple_of(b * part + i * size, size), size), :] = total.astype(BF16)
                    return carry
                lax.fori_loop(0, part // size, body, 0)
            for name in ("out_p", "out_m", "out_c", "own"):
                cp[name]().start()
        elif step == 5:
            cp["out_p"]().wait_recv()
            cp["fwd_a"]().start()
            cp["cor_p"]().start()
            cp["out_m"]().wait_recv()
            cp["fwd_b"]().start()
            cp["cor_m"]().start()
        elif step == 6:
            cp["fwd_a"]().wait_recv()
            cp["fwd_b"]().wait_recv()
            cp["cor_f"]().start()
        elif step == 7:
            for name in ("out_c", "cor_p", "cor_m", "cor_f"):
                cp[name]().wait_recv()
            cp["own"]().wait()

    hops = nz // 2
    events = []
    for h in range(hops + 1):
        events.append((h - 0.5, 2 * nc, h))
    for k in range(2 * nc):
        for h in range(hops + 1):
            events.append((h if k == 0 else 2 * k + h + 1, k, h))
    events.sort()
    last_x = -1
    for _, k, h in events:
        z_step(k, h)
        if h == hops:
            if k == 2 * nc:
                build_tables()
            else:
                dispatch(k)
                if k >= 2 and k - 2 < nc + 1:
                    arrive(k - 2)
                    last_x = k - 2
                    if last_x == nc - 1:
                        make_hidden()
    back = 0
    for k in range(last_x + 1, 2 * nc):
        arrive(k)
        if k == nc - 1:
            make_hidden()
        if k >= 2 * nc - 2:
            send_back(back)
            back += 1
    do_y = ny > 1
    if do_y:
        y_step(0, 1)
    make_pre_grad()
    for c in range(nc):
        g_up[c * cw:(c + 1) * cw, :] = mm(xrecv[c], pgr[...], 0, 0).astype(BF16)
    if do_y:
        y_step(1, 1)
        y_step(0, 2)
    ys = [(0, 3), (1, 2), (0, 4), (1, 3), (0, 5), (1, 4), (0, 6), (1, 5), (0, 7), (1, 6), (1, 7)]
    if not do_y:
        ys = []
    s_events = []
    for m in range(2 * nc):
        if back < 2 * nc:
            send_back(back)
            back += 1
        combine(m)
        if ys:
            y_step(*ys.pop(0))
        if m >= 1:
            s_step(m - 1, 1)
            s_step(m - 1, 2)
        if m >= 2:
            for h in range(3, hops + 1):
                s_step(m - 2, h)
    last = 2 * nc - 1
    for h in range(3, hops + 1):
        s_step(last - 1, h)
    if ys:
        y_step(*ys.pop(0))
    for h in range(1, hops + 1):
        s_step(last, h)
        if ys:
            y_step(*ys.pop(0))
    while ys:
        y_step(*ys.pop(0))

    for k in range(2 * nc + 1):
        for way in (0, 1):
            for h in range(1, ways(k)[way] + 1):
                z_copy(k, way, h).wait_send()
    for k in range(2 * nc):
        for j in range(1, nx):
            x_copy(k, j).wait_send()
            c_copy(k, j).wait_send()
        for way in (0, 1):
            for h in range(1, ways(k)[way] + 1):
                s_copy(k, way, h).wait_send()
    if do_y:
        for w in (0, 1):
            for name, cp in y_copies(w).items():
                if name != "own":
                    cp().wait_send()


def run(cfg, tokens, expert_ids, gate_weights, up_weight, down_weight, out_grad):
    tok, width, hid_w, nc, cw = cfg.tok, cfg.width, cfg.hidden, cfg.nc, cfg.cw
    rows, rx, seen, nz, nx = cfg.rows, cfg.rows_x, cfg.seen, cfg.nz, cfg.nx
    vmem = pl.BlockSpec(memory_space=pltpu.VMEM)
    anywhere = pl.BlockSpec(memory_space=pl.ANY)
    dma = pltpu.SemaphoreType.DMA
    scratch = [
        pltpu.VMEM((2 * nc, seen, cw), BF16),
        pltpu.VMEM((seen, 128), BF16),
        pltpu.VMEM((2 * nc, rows - rx, cw), BF16),
        pltpu.VMEM((2 * nc, rows, cw), BF16),
        pltpu.VMEM((width, hid_w), BF16),
        pltpu.VMEM((hid_w, width), BF16),
        pltpu.VMEM((rows, hid_w), F32),
        pltpu.VMEM((rows, hid_w), F32),
        pltpu.VMEM((rows, hid_w), BF16),
        pltpu.VMEM((rows, hid_w), BF16),
        pltpu.VMEM((rows, seen), BF16),
        pltpu.VMEM((seen, rows), BF16),
        pltpu.VMEM((rows, 128), F32),
        pltpu.VMEM((2 * nc, rows - rx, cw), BF16),
        pltpu.VMEM((2 * nc, rows, cw), BF16),
        pltpu.VMEM((2 * nc, seen, cw), BF16),
        pltpu.VMEM((2 * nc, nz - 1, tok, cw), BF16),
        pltpu.VMEM((2 * nc, tok, cw), F32),
        pltpu.VMEM((hid_w, width), BF16),
        pltpu.VMEM((width, hid_w), BF16),
        pltpu.VMEM((hid_w // 2, width), BF16),
        pltpu.VMEM((width // 2, hid_w), BF16),
        pltpu.VMEM((6, hid_w // 16, width), BF16),
        pltpu.VMEM((6, width // 16, hid_w), BF16),
        pltpu.VMEM((hid_w // 8, width), BF16),
        pltpu.VMEM((width // 8, hid_w), BF16),
        dma((2,)),
        dma((2 * nc + 1, nz - 1)),
        dma((2 * nc + 1, nz - 1)),
        dma((2 * nc, nx - 1)),
        dma((2 * nc, nx - 1)),
        dma((2 * nc, nx - 1)),
        dma((2 * nc, nx - 1)),
        dma((2 * nc, nz - 1)),
        dma((2 * nc, nz - 1)),
        dma((2, 15)),
        dma((2, 15)),
        dma((2,)),
    ]
    return pl.pallas_call(
        functools.partial(kernel, cfg),
        out_shape=(
            jax.ShapeDtypeStruct((tok, width), BF16),
            jax.ShapeDtypeStruct((tok, width), BF16),
            jax.ShapeDtypeStruct((1, width, hid_w), BF16),
            jax.ShapeDtypeStruct((1, hid_w, width), BF16),
        ),
        in_specs=[vmem, vmem, vmem, vmem, anywhere, anywhere],
        out_specs=(vmem, vmem, anywhere, anywhere),
        scratch_shapes=scratch,
        compiler_params=pltpu.CompilerParams(
            collective_id=0, has_side_effects=True, vmem_limit_bytes=60 * 2**20
        ),
        name="expert_layer",
    )(tokens, out_grad, expert_ids, gate_weights, up_weight, down_weight)


def solution(mesh):
    dp, experts = mesh.shape["dp"], mesh.shape["expert"]

    def shards(tokens, expert_ids, gate_weights, up_weight, down_weight, out_grad):
        cfg = Cfg(8, experts // 8, dp // 2, tokens.shape[0], expert_ids.shape[1], tokens.shape[1],
                  up_weight.shape[2], 4)
        return run(cfg, tokens, expert_ids, gate_weights, up_weight, down_weight, out_grad)

    return jax.shard_map(
        shards,
        mesh=mesh,
        in_specs=(
            P(("dp", "expert"), None),
            P(("dp", "expert"), None),
            P(("dp", "expert"), None),
            P("expert", None, None),
            P("expert", None, None),
            P(("dp", "expert"), None),
        ),
        out_specs=(
            P(("dp", "expert"), None),
            P(("dp", "expert"), None),
            P("expert", None, None),
            P("expert", None, None),
        ),
        check_vma=False,
    )
```

time: 421 us -> 199 us (0.47)
  waiting for transfers between devices: 241 us -> 0 us
  Pallas kernels: 0 us -> 184 us
  other arithmetic: 48.4 us -> 0 us
  local copies, waits for them, and re-layouts: 57.6 us -> 11.6 us
  starting transfers between devices: 33.9 us -> 0 us
  matrix products: 24.1 us -> 0 us
  between operations: 14.2 us -> 0.64 us
    all_to_all x4 -> x0, waiting for transfers between devices: 218 us -> none  [the longest x1 56.4 us: shards(): lax.all_to_all(send_x, 'expert', split_axis=0, concat_axis=0, tiled=True)]
    pallas_call x0 -> x1, Pallas kernels: none -> 184 us  [run(): pl.pallas_call(functools.partial(kernel, cfg), out_shape=(jax.ShapeDtypeS...]
    all_to_all x4 -> x0, starting transfers between devices: 33.6 us -> none  [the longest x1 12.3 us: shards(): lax.all_to_all(send_x, 'expert', split_axis=0, concat_axis=0, tiled=True)]
    gather x5 -> x0, other arithmetic: 30.3 us -> none  [the longest x3 30.3 us: shards(): jnp.repeat(jnp.arange(tok_count, dtype=jnp.int32), top_count, total_repea...]
    reshape x9 -> x0, local copies, waits for them, and re-layouts: 30.1 us -> none  [the longest x1 4.4 us: shards(): dy_rows = got_dy.reshape(recv_rows, model_width)]
    dot_general x6 -> x0, matrix products: 24.1 us -> none  [the longest x4 16.1 us: contract(): lax.dot_general(left, right, (((left_dim,), (right_dim,)), ((), ())), pre...]
    psum x1 -> x0, waiting for transfers between devices: 22.6 us -> none  [shards(): lax.psum(up_grad.astype(jnp.bfloat16), 'dp').astype(jnp.float32)]
    scatter x1 -> x0, local copies, waits for them, and re-layouts: 10.9 us -> none  [shards(): jnp.zeros((recv_rows, model_width), jnp.bfloat16).at[target]]
  transfers between devices with their start and end apart: 5 -> 0, of which waited for: 5 -> 0; matrix products, arithmetic and copies ran while one was open for 17% -> 0% of each run, Pallas kernels for 0% -> 0%
where the time goes in v1:
time: 199 us; the launch traced here: 196 us
  Pallas kernels  184 us (92%)
  local copies, waits for them, and re-layouts  11.6 us (6%)
    pallas_call x1, Pallas kernels, run(): pl.pallas_call(functools.partial(kernel, cfg), out_shape=(jax.ShapeDtypeS...  184 us
    unnamed x8, local copies, waits for them, and re-layouts  11.6 us

profile of v1, /device:TPU:1, one launch (start us, length us, event | category | flops | bytes accessed | tf_op | source)
XLA Modules:
  0.0 195.9 jit_solution(2013466272730337581)
XLA Ops:
  0.6 1.4 copy.10.refs_2_
  2.0 1.4 copy.11.refs_3_
  3.4 183.7 %expert_layer.1 = (bf16[48,2048]{1,0:T(8,128)(2,1)}, bf16[48,2048]{1,0:T(8,128)(2,1)}, bf16[1,2048,768]{2,1,0:T(8,128)(2,1)}, bf16[1,768,2048]{2,1,0:T(8,128)(2,1)}) custom-call(bf16[48,2048]{1,0:T(8,128)(2,1)} %refs_0_.1, bf16[48,2048]{1,0:T(8,128)(2,1)} %refs_1_.1, s32[48,8]{1,0:T(8,128)} %copy.10.refs_2_, f32[48,8]{1,0:T(8,128)} %copy.11.refs_3_, ...), custom_call_target="tpu_custom_call" | custom-call | tf_op jit(solution)/shard_map/expert_layer/pallas_call | solution.py:492
  187.1 1.6 copy.16
  188.7 1.6 copy.17
  190.3 0.0 copy-start
  190.3 3.9 %copy.18 = bf16[1,2048,768]{2,1,0:T(8,128)(2,1)} copy(bf16[1,2048,768]{2,1,0:T(8,128)(2,1)} %get-tuple-element.10) | data formatting | bytes 6291456
  194.2 0.0 copy-done
  194.2 1.7 copy.19
Async XLA Ops:
  190.3 3.9 %copy-start = (bf16[1,768,2048]{2,1,0:T(8,128)(2,1)S(1)}, bf16[1,768,2048]{2,1,0:T(8,128)(2,1)}, u32[]{:S(2)}) copy-start(bf16[1,768,2048]{2,1,0:T(8,128)(2,1)} %get-tuple-element.11) | copy-start | bytes 9437188

commit v2 on v1

--- a/solution.py
+++ b/solution.py
@@ -10,6 +10,7 @@
 BF16 = jnp.bfloat16
 F32 = jnp.float32
 MESH_ID = pl.DeviceIdType.MESH
+LAG = 2
 
 
 def mm(left, right, left_dim=1, right_dim=0):
@@ -60,6 +61,14 @@
             src_ref=src, dst_ref=dst, send_sem=ss, recv_sem=rs, device_id=to, device_id_type=MESH_ID
         )
 
+    own_block = []
+    for k in range(2 * nc):
+        c = k % nc
+        source = tok_ref if k < nc else og_ref
+        own_block.append(pltpu.make_async_copy(
+            source.at[:, pl.ds(c * cw, cw)], zbuf.at[k, pl.ds(0, tok)], w_sem.at[2 + k]))
+    for load in own_block:
+        load.start()
     w_up = pltpu.make_async_copy(up_hbm.at[0], upv, w_sem.at[0])
     w_down = pltpu.make_async_copy(down_hbm.at[0], downv, w_sem.at[1])
     w_up.start()
@@ -72,31 +81,34 @@
     for partner in partners:
         pl.semaphore_signal(barrier, inc=1, device_id=partner, device_id_type=MESH_ID)
 
-    for k in range(nc):
-        zbuf[k, 0:tok, :] = tok_ref[:, k * cw:(k + 1) * cw]
-        zbuf[nc + k, 0:tok, :] = og_ref[:, k * cw:(k + 1) * cw]
+    top = cfg.top
+    gate = gate_ref[...]
+    high = gate.astype(BF16).astype(F32)
+    rest = gate - high
+    middle = rest.astype(BF16).astype(F32)
+    low = rest - middle
+    stack = jnp.concatenate([ids_ref[...].astype(F32), high, middle, low], axis=0).astype(BF16)
+    row_e = lax.broadcasted_iota(jnp.int32, (4 * top, 4 * top), 0)
+    col_e = lax.broadcasted_iota(jnp.int32, (4 * top, 4 * top), 1)
+    turned = mm(stack, jnp.where(row_e == col_e, 1.0, 0.0).astype(BF16), 0, 0)
     lane = lax.broadcasted_iota(jnp.int32, (tok, 128), 1)
-    lane_e = lane & (experts - 1)
+    lane_e = (lane & (experts - 1)).astype(F32)
     hit = jnp.zeros((tok, 128), F32)
-    gate = jnp.zeros((tok, 128), F32)
-    for k in range(cfg.top):
-        match = ids_ref[:, k:k + 1] == lane_e
+    split = jnp.zeros((tok, 128), F32)
+    for k in range(top):
+        match = turned[:, k:k + 1] == lane_e
         hit = hit + jnp.where(match, 1.0, 0.0)
-        gate = gate + jnp.where(match, gate_ref[:, k:k + 1], 0.0)
+        value = jnp.where(
+            lane < 2 * experts, turned[:, top + k:top + k + 1],
+            jnp.where(lane < 3 * experts, turned[:, 2 * top + k:2 * top + k + 1],
+                      turned[:, 3 * top + k:3 * top + k + 1]))
+        split = split + jnp.where(match, value, 0.0)
     row_t = lax.broadcasted_iota(jnp.int32, (tok, tok), 0)
     col_t = lax.broadcasted_iota(jnp.int32, (tok, tok), 1)
     earlier = jnp.where(col_t < row_t, 1.0, 0.0).astype(BF16)
     before = mm(earlier, hit.astype(BF16))
     place = jnp.where(hit > 0.5, before, -1.0)
-    high = gate.astype(BF16).astype(F32)
-    rest = gate - high
-    middle = rest.astype(BF16).astype(F32)
-    low = rest - middle
-    table = jnp.where(
-        lane < experts, place,
-        jnp.where(lane < 2 * experts, high,
-                  jnp.where(lane < 3 * experts, middle,
-                            jnp.where(lane < 4 * experts, low, 0.0))))
+    table = jnp.where(lane < experts, place, jnp.where(lane < 4 * experts, split, 0.0))
     zmeta[0:tok, :] = table.astype(BF16)
 
     pl.semaphore_wait(barrier, len(partners))
@@ -180,7 +192,8 @@
                 lin[...] = part
             else:
                 lin[...] += part
-            g_down[:, c * cw:(c + 1) * cw] = mm(hid[...], xrecv[k], 0, 0).astype(BF16)
+            at = c % (nc // 2) * cw
+            g_down[c // (nc // 2), :, at:at + cw] = mm(hid[...], xrecv[k], 0, 0).astype(BF16)
 
     blk = 16
 
@@ -258,19 +271,29 @@
         pbuf[m, tok:, :] = part[tok:].astype(BF16)
         s_step(m, 0)
 
-    mats = [(g_down, c_down, r_down, f_down, gdown_ref), (g_up, c_up, r_up, f_up, gup_ref)]
+    pieces = [
+        (g_down.at[0], c_down.at[0], r_down.at[0], f_down.at[0]),
+        (g_down.at[1], c_down.at[1], r_down.at[1], f_down.at[1]),
+        (g_up.at[0], c_up.at[0], r_up.at[0], f_up.at[0]),
+        (g_up.at[1], c_up.at[1], r_up.at[1], f_up.at[1]),
+    ]
+
+    def y_sizes(w):
+        half = pieces[w][0].shape[0] // 2
+        return half, half // 4, half // 8
 
     def y_copies(w):
-        g, cr, r, f, out = mats[w]
-        half = g.shape[0] // 2
-        shard = half // 4
-        part = shard // 2
+        g, cr, r, f = pieces[w]
+        half, shard, part = y_sizes(w)
 
         def of(step, b=0):
             return pl.multiple_of(lax.rem(y + step + ny, ny) * shard + b * part, part)
 
         def final(step, b, count):
-            return out.at[0, pl.ds(pl.multiple_of(core * half + of(step, b), part), count)]
+            first = core * half + of(step, b)
+            if w < 2:
+                return gdown_ref.at[0, pl.ds(pl.multiple_of(first, part), count), pl.ds(w * (width // 2), width // 2)]
+            return gup_ref.at[0, pl.ds(pl.multiple_of((w - 2) * (width // 2) + first, part), count)]
 
         def sem(i):
             return y_ss.at[w, i], y_rs.at[w, i]
@@ -305,10 +328,8 @@
         lax.fori_loop(0, count // size, body, 0)
 
     def y_step(w, step):
-        g, cr, r, f, out = mats[w]
-        half = g.shape[0] // 2
-        shard = half // 4
-        part = shard // 2
+        g, cr, r, f = pieces[w]
+        half, shard, part = y_sizes(w)
         cp = y_copies(w)
 
         def of(move, b=0):
@@ -359,71 +380,87 @@
             cp["own"]().wait()
 
     hops = nz // 2
+    do_y = ny > 1
+    per = nc // 2
+
+    def y_run(*steps):
+        if do_y:
+            for w, step in steps:
+                y_step(w, step)
+
+    def weight_grad_up(p):
+        for c in range(p * per, (p + 1) * per):
+            at = (c - p * per) * cw
+            g_up[p, at:at + cw, :] = mm(xrecv[c], pgr[...], 0, 0).astype(BF16)
+
+    def arrived(k):
+        arrive(k)
+        if k == nc - 1:
+            make_hidden()
+        if k == nc + per - 1:
+            y_run((0, 1))
+
     events = []
     for h in range(hops + 1):
         events.append((h - 0.5, 2 * nc, h))
     for k in range(2 * nc):
         for h in range(hops + 1):
-            events.append((h if k == 0 else 2 * k + h + 1, k, h))
+            events.append((h if k == 0 else k + h + 1, k, h))
     events.sort()
-    last_x = -1
     for _, k, h in events:
+        if h == 0 and k < 2 * nc:
+            own_block[k].wait()
         z_step(k, h)
         if h == hops:
             if k == 2 * nc:
                 build_tables()
             else:
                 dispatch(k)
-                if k >= 2 and k - 2 < nc + 1:
-                    arrive(k - 2)
-                    last_x = k - 2
-                    if last_x == nc - 1:
-                        make_hidden()
+                if k >= LAG:
+                    arrived(k - LAG)
     back = 0
-    for k in range(last_x + 1, 2 * nc):
-        arrive(k)
-        if k == nc - 1:
-            make_hidden()
+    for k in range(2 * nc - LAG, 2 * nc):
         if k >= 2 * nc - 2:
             send_back(back)
             back += 1
-    do_y = ny > 1
-    if do_y:
-        y_step(0, 1)
+        arrived(k)
+    y_run((1, 1), (0, 2))
+    send_back(back)
+    back += 1
     make_pre_grad()
-    for c in range(nc):
-        g_up[c * cw:(c + 1) * cw, :] = mm(xrecv[c], pgr[...], 0, 0).astype(BF16)
-    if do_y:
-        y_step(1, 1)
-        y_step(0, 2)
-    ys = [(0, 3), (1, 2), (0, 4), (1, 3), (0, 5), (1, 4), (0, 6), (1, 5), (0, 7), (1, 6), (1, 7)]
-    if not do_y:
-        ys = []
-    s_events = []
-    for m in range(2 * nc):
-        if back < 2 * nc:
+    weight_grad_up(0)
+    y_run((2, 1), (0, 3))
+    send_back(back)
+    back += 1
+    weight_grad_up(1)
+    y_run((3, 1), (1, 2))
+    plan = [
+        [(0, 4), (2, 2)],
+        [(1, 3), (3, 2)],
+        [(0, 5), (1, 4)],
+        [(2, 3), (0, 6)],
+        [(1, 5), (2, 4), (3, 3)],
+        [(1, 6), (2, 5), (3, 4)],
+        [(2, 6), (3, 5), (0, 7)],
+        [(3, 6), (1, 7)],
+        [],
+        [(2, 7)],
+        [],
+        [(3, 7)],
+    ]
+    count = 2 * nc
+    for m in range(count + hops):
+        if back < count:
             send_back(back)
             back += 1
-        combine(m)
-        if ys:
-            y_step(*ys.pop(0))
-        if m >= 1:
-            s_step(m - 1, 1)
-            s_step(m - 1, 2)
-        if m >= 2:
-            for h in range(3, hops + 1):
-                s_step(m - 2, h)
-    last = 2 * nc - 1
-    for h in range(3, hops + 1):
-        s_step(last - 1, h)
-    if ys:
-        y_step(*ys.pop(0))
-    for h in range(1, hops + 1):
-        s_step(last, h)
-        if ys:
-            y_step(*ys.pop(0))
-    while ys:
-        y_step(*ys.pop(0))
+        if m < count:
+            combine(m)
+        for h in range(hops, 0, -1):
+            if 0 <= m - h < count:
+                s_step(m - h, h)
+        if m < len(plan):
+            y_run(*plan[m])
+    y_run(*[step for late in plan[count + hops:] for step in late])
 
     for k in range(2 * nc + 1):
         for way in (0, 1):
@@ -437,10 +474,47 @@
             for h in range(1, ways(k)[way] + 1):
                 s_copy(k, way, h).wait_send()
     if do_y:
-        for w in (0, 1):
+        for w in range(4):
             for name, cp in y_copies(w).items():
                 if name != "own":
                     cp().wait_send()
+
+
+def hand_out(results):
+    anywhere = pl.BlockSpec(memory_space=pl.ANY)
+    count = len(results)
+    parts = 4
+
+    def body(*refs):
+        held, sems = refs[2 * count:3 * count], refs[3 * count]
+        moves = []
+        for i in range(count):
+            pieces = parts if len(results[i].shape) == 3 else 1
+            size = results[i].shape[-2] // pieces
+            for p in range(pieces):
+                at = (pl.ds(p * size, size),)
+                if len(results[i].shape) == 3:
+                    at = (0,) + at
+                moves.append((
+                    pltpu.make_async_copy(refs[i].at[at], held[i].at[at], sems.at[0, i, p]),
+                    pltpu.make_async_copy(held[i].at[at], refs[count + i].at[at], sems.at[1, i, p])))
+        for load, _ in moves:
+            load.start()
+        for load, store in moves:
+            load.wait()
+            store.start()
+        for _, store in moves:
+            store.wait()
+
+    return pl.pallas_call(
+        body,
+        out_shape=tuple(jax.ShapeDtypeStruct(r.shape, r.dtype) for r in results),
+        in_specs=[anywhere] * count,
+        out_specs=(anywhere,) * count,
+        scratch_shapes=[pltpu.VMEM(r.shape, r.dtype) for r in results] + [pltpu.SemaphoreType.DMA((2, count, parts))],
+        compiler_params=pltpu.CompilerParams(vmem_limit_bytes=60 * 2**20),
+        name="hand_out",
+    )(*results)
 
 
 def run(cfg, tokens, expert_ids, gate_weights, up_weight, down_weight, out_grad):
@@ -468,15 +542,15 @@
         pltpu.VMEM((2 * nc, seen, cw), BF16),
         pltpu.VMEM((2 * nc, nz - 1, tok, cw), BF16),
         pltpu.VMEM((2 * nc, tok, cw), F32),
-        pltpu.VMEM((hid_w, width), BF16),
-        pltpu.VMEM((width, hid_w), BF16),
-        pltpu.VMEM((hid_w // 2, width), BF16),
-        pltpu.VMEM((width // 2, hid_w), BF16),
-        pltpu.VMEM((6, hid_w // 16, width), BF16),
-        pltpu.VMEM((6, width // 16, hid_w), BF16),
-        pltpu.VMEM((hid_w // 8, width), BF16),
-        pltpu.VMEM((width // 8, hid_w), BF16),
-        dma((2,)),
+        pltpu.VMEM((2, hid_w, width // 2), BF16),
+        pltpu.VMEM((2, width // 2, hid_w), BF16),
+        pltpu.VMEM((2, hid_w // 2, width // 2), BF16),
+        pltpu.VMEM((2, width // 4, hid_w), BF16),
+        pltpu.VMEM((2, 6, hid_w // 16, width // 2), BF16),
+        pltpu.VMEM((2, 6, width // 32, hid_w), BF16),
+        pltpu.VMEM((2, hid_w // 8, width // 2), BF16),
+        pltpu.VMEM((2, width // 16, hid_w), BF16),
+        dma((2 + 2 * nc,)),
         dma((2 * nc + 1, nz - 1)),
         dma((2 * nc + 1, nz - 1)),
         dma((2 * nc, nx - 1)),
@@ -485,11 +559,11 @@
         dma((2 * nc, nx - 1)),
         dma((2 * nc, nz - 1)),
         dma((2 * nc, nz - 1)),
-        dma((2, 15)),
-        dma((2, 15)),
-        dma((2,)),
+        dma((4, 15)),
+        dma((4, 15)),
+        dma((4,)),
     ]
-    return pl.pallas_call(
+    results = pl.pallas_call(
         functools.partial(kernel, cfg),
         out_shape=(
             jax.ShapeDtypeStruct((tok, width), BF16),
@@ -497,14 +571,15 @@
             jax.ShapeDtypeStruct((1, width, hid_w), BF16),
             jax.ShapeDtypeStruct((1, hid_w, width), BF16),
         ),
-        in_specs=[vmem, vmem, vmem, vmem, anywhere, anywhere],
+        in_specs=[anywhere, anywhere, vmem, vmem, anywhere, anywhere],
         out_specs=(vmem, vmem, anywhere, anywhere),
         scratch_shapes=scratch,
         compiler_params=pltpu.CompilerParams(
             collective_id=0, has_side_effects=True, vmem_limit_bytes=60 * 2**20
         ),
         name="expert_layer",
-    )(tokens, out_grad, expert_ids, gate_weights, up_weight, down_weight)
+    )(tokens, out_grad, expert_ids.T, gate_weights.T, up_weight, down_weight)
+    return hand_out(results)
 
 
 def solution(mesh):

time: 199 us -> 164 us (0.82)
  the two profiles are of different devices: /device:TPU:1 before, /device:TPU:16 now
where the time goes in v2:
time: 164 us
  Pallas kernels  163 us (99%)
    pallas_call x1, Pallas kernels, run(): pl.pallas_call(functools.partial(kernel, cfg), out_shape=(jax.ShapeDtypeS...  158 us
    pallas_call x1, Pallas kernels, hand_out(): pl.pallas_call(body, out_shape=tuple((jax.ShapeDtypeStruct(r.shape, r.dty...  5.72 us

profile of v2, /device:TPU:16, one launch (start us, length us, event | category | flops | bytes accessed | tf_op | source)
XLA Modules:
  0.0 164.1 jit_solution(9271653211168296260)
XLA Ops:
  0.6 157.6 %expert_layer.1 = (bf16[48,2048]{1,0:T(8,128)(2,1)}, bf16[48,2048]{1,0:T(8,128)(2,1)}, bf16[1,2048,768]{2,1,0:T(8,128)(2,1)}, bf16[1,768,2048]{2,1,0:T(8,128)(2,1)}) custom-call(bf16[48,2048]{1,0:T(8,128)(2,1)} %refs_0_.1, bf16[48,2048]{1,0:T(8,128)(2,1)} %refs_1_.1, s32[8,48]{1,0:T(8,128)} %bitcast.2, f32[8,48]{1,0:T(8,128)} %bitcast.3, ...), custom_call_target="tpu_custom_call" | custom-call | tf_op jit(solution)/shard_map/expert_layer/pallas_call | solution.py:566
  158.2 5.7 %hand_out.1 = (bf16[48,2048]{1,0:T(8,128)(2,1)}, bf16[48,2048]{1,0:T(8,128)(2,1)}, bf16[1,2048,768]{2,1,0:T(8,128)(2,1)}, bf16[1,768,2048]{2,1,0:T(8,128)(2,1)}) custom-call(bf16[48,2048]{1,0:T(8,128)(2,1)} %get-tuple-element.8.refs_0_, bf16[48,2048]{1,0:T(8,128)(2,1)} %get-tuple-element.9.refs_1_, bf16[1,2048,768]{2,1,0:T(8,128)(2,1)} %get-tuple-element.10.refs_2_, ...), custom_call_target="tpu_custom_call" | custom-call | tf_op jit(solution)/shard_map/hand_out/pallas_call | solution.py:509

commit v3 on v2

--- a/solution.py
+++ b/solution.py
@@ -11,6 +11,9 @@
 F32 = jnp.float32
 MESH_ID = pl.DeviceIdType.MESH
 LAG = 2
+FIRST = 0.5
+STRAIGHT = 1
+AHEAD = 2
 
 
 def mm(left, right, left_dim=1, right_dim=0):
@@ -74,7 +77,7 @@
     w_up.start()
     w_down.start()
 
-    partners = [at_z(1), at_z(-1)] + [at_x(j) for j in range(1, nx)]
+    partners = [at_z(d) for d in range(1, nz)] + [at_x(j) for j in range(1, nx)]
     if ny > 1:
         partners += [at_y(1), at_y(-1), other_core]
     barrier = pltpu.get_barrier_semaphore()
@@ -120,10 +123,22 @@
     def z_copy(k, way, hop):
         source = hop - 1 if way == 0 else (nz - hop + 1) % nz
         target = hop if way == 0 else nz - hop
-        buf = zmeta if k == 2 * nc else zbuf.at[k]
         return copy(
-            buf.at[pl.ds(source * tok, tok)], buf.at[pl.ds(target * tok, tok)],
+            zbuf.at[k, pl.ds(source * tok, tok)], zbuf.at[k, pl.ds(target * tok, tok)],
             z_ss.at[k, target - 1], z_rs.at[k, target - 1], at_z(1 if way == 0 else -1))
+
+    hw = cw // 2
+    direct = sorted(range(1, nz), key=lambda d: -min(d, nz - d))
+
+    def z_direct(part, d):
+        if part == 2:
+            return copy(
+                zmeta.at[pl.ds(0, tok)], zmeta.at[pl.ds(d * tok, tok)],
+                z_ss.at[2 * nc + 1, d - 1], z_rs.at[2 * nc + 1, d - 1], at_z(d))
+        row, cols = (0 if part == 0 else 2 * nc), pl.ds(part * hw, hw)
+        return copy(
+            zbuf.at[0, pl.ds(0, tok), cols], zbuf.at[0, pl.ds(d * tok, tok), cols],
+            z_ss.at[row, d - 1], z_rs.at[row, d - 1], at_z(d))
 
     def z_step(k, hop):
         for way in (0, 1):
@@ -149,6 +164,8 @@
             hot = hot + jnp.where(place_lane == value, 1.0, 0.0)
         onehot_t[...] = hot[:, 0:rows].astype(BF16)
         onehot[...] = hot.T[0:rows].astype(BF16)
+
+    def build_gates():
         picked = mm(onehot[...], zmeta[...])
         lanes_r = lax.broadcasted_iota(jnp.int32, (rx, 128), 1)
         for j in range(nx):
@@ -157,24 +174,28 @@
             value = jnp.sum(jnp.where(mine, picked[j * rx:(j + 1) * rx], 0.0), axis=1, keepdims=True)
             gates[j * rx:(j + 1) * rx, :] = jnp.broadcast_to(value, (rx, 128))
 
-    def x_copy(k, j):
+    def x_copy(k, j, part=None):
+        row = 2 * nc if part == 1 else k
+        cols = pl.ds(0, cw) if part is None else pl.ds(part * hw, hw)
         return copy(
-            xsend.at[k, pl.ds((j - 1) * rx, rx)], xrecv.at[k, pl.ds(j * rx, rx)],
-            x_ss.at[k, j - 1], x_rs.at[k, j - 1], at_x(j))
-
-    def dispatch(k):
-        packed = mm(onehot[...], zbuf[k])
+            xsend.at[k, pl.ds((j - 1) * rx, rx), cols], xrecv.at[k, pl.ds(j * rx, rx), cols],
+            x_ss.at[row, j - 1], x_rs.at[row, j - 1], at_x(j))
+
+    def dispatch(k, part=None):
+        cols = slice(0, cw) if part is None else slice(part * hw, (part + 1) * hw)
+        packed = mm(onehot[...], zbuf[k, :, cols])
         if k >= nc:
             packed = packed * gates[:, 0:1]
         packed = packed.astype(BF16)
-        xsend[k] = packed[rx:]
-        xrecv[k, 0:rx, :] = packed[0:rx]
+        xsend[k, :, cols] = packed[rx:]
+        xrecv[k, 0:rx, cols] = packed[0:rx]
         for j in range(1, nx):
-            x_copy(k, j).start()
+            x_copy(k, j, part).start()
 
     def arrive(k):
         for j in range(1, nx):
-            x_copy(k, j).wait_recv()
+            for part in (0, 1) if k == 0 else (None,):
+                x_copy(k, j, part).wait_recv()
         if k < nc:
             if k == 0:
                 w_up.wait()
@@ -195,7 +216,7 @@
             at = c % (nc // 2) * cw
             g_down[c // (nc // 2), :, at:at + cw] = mm(hid[...], xrecv[k], 0, 0).astype(BF16)
 
-    blk = 16
+    blk = 48
 
     def make_hidden():
         def body(i, carry):
@@ -214,10 +235,14 @@
             return carry
         lax.fori_loop(0, rows // blk, body, 0)
 
-    def c_copy(m, j):
+    last = 2 * nc - 1
+
+    def c_copy(m, j, part=None):
+        row = 2 * nc if part == 1 else m
+        cols = pl.ds(0, cw) if part is None else pl.ds(part * hw, hw)
         return copy(
-            csend.at[m, pl.ds((j - 1) * rx, rx)], crecv.at[m, pl.ds(j * rx, rx)],
-            c_ss.at[m, j - 1], c_rs.at[m, j - 1], at_x(-j))
+            csend.at[m, pl.ds((j - 1) * rx, rx), cols], crecv.at[m, pl.ds(j * rx, rx), cols],
+            c_ss.at[row, j - 1], c_rs.at[row, j - 1], at_x(-j))
 
     def send_back(m):
         c = m % nc
@@ -228,8 +253,9 @@
         out = out.astype(BF16)
         csend[m] = out[rx:]
         crecv[m, 0:rx, :] = out[0:rx]
-        for j in range(1, nx):
-            c_copy(m, j).start()
+        for part in (0, 1) if m == last else (None,):
+            for j in range(1, nx):
+                c_copy(m, j, part).start()
 
     def s_copy(m, way, hop):
         plus, minus = ways(m)
@@ -260,16 +286,39 @@
             target = mixed_ref if m < nc else gtok_ref
             target[:, c * cw:(c + 1) * cw] = fin[m].astype(BF16)
 
-    def combine(m):
+    def combine(m, part=None):
+        cols = slice(0, cw) if part is None else slice(part * hw, (part + 1) * hw)
         for j in range(1, nx):
-            c_copy(m, j).wait_recv()
-        got = crecv[m]
+            c_copy(m, j, part).wait_recv()
+        got = crecv[m, :, cols]
         if m < nc:
             got = (got.astype(F32) * gates[:, 0:1]).astype(BF16)
-        part = mm(onehot_t[...], got)
-        fin[m] = part[0:tok]
-        pbuf[m, tok:, :] = part[tok:].astype(BF16)
-        s_step(m, 0)
+        total = mm(onehot_t[...], got)
+        fin[m, :, cols] = total[0:tok]
+        pbuf[m, tok:, cols] = total[tok:].astype(BF16)
+        if m < ring:
+            s_step(m, 0)
+        else:
+            for d in direct:
+                s_direct(m, part, d).start()
+
+    ring = 2 * nc - STRAIGHT
+
+    def s_direct(m, part, d):
+        row = 2 * nc if part == 1 else m
+        cols = pl.ds(0, cw) if part is None else pl.ds(part * hw, hw)
+        return copy(
+            pbuf.at[m, pl.ds(d * tok, tok), cols], rsbuf.at[m, d - 1, slice(None), cols],
+            s_ss.at[row, d - 1], s_rs.at[row, d - 1], at_z(-d))
+
+    def finish(m, part=None):
+        cols = slice(0, cw) if part is None else slice(part * hw, (part + 1) * hw)
+        total = fin[m, :, cols]
+        for d in range(1, nz):
+            s_direct(m, part, d).wait_recv()
+            total = total + rsbuf[m, d - 1, :, cols].astype(F32)
+        at = m % nc * cw + cols.start
+        gtok_ref[:, at:at + cols.stop - cols.start] = total.astype(BF16)
 
     pieces = [
         (g_down.at[0], c_down.at[0], r_down.at[0], f_down.at[0]),
@@ -318,7 +367,7 @@
         )
 
     def add_rows(target, t0, source, s0, count, extra=None):
-        size = 16 if count % 16 == 0 else count
+        size = 64 if count % 64 == 0 else count
 
         def body(i, carry):
             a = pl.ds(pl.multiple_of(t0 + i * size, size), size)
@@ -352,7 +401,7 @@
         elif step == 4:
             for name in ("near_a", "near_b", "two_a", "two_b"):
                 cp[name]().wait_recv()
-            size = 16 if part % 16 == 0 else part
+            size = 64 if part % 64 == 0 else part
             for b, near, two in ((0, 3, 4), (1, 2, 5)):
                 def body(i, carry):
                     a = pl.ds(pl.multiple_of(i * size, size), size)
@@ -400,24 +449,34 @@
         if k == nc + per - 1:
             y_run((0, 1))
 
-    events = []
-    for h in range(hops + 1):
-        events.append((h - 0.5, 2 * nc, h))
-    for k in range(2 * nc):
+    own_block[0].wait()
+    for part in (2, 0, 1):
+        for d in direct:
+            z_direct(part, d).start()
+    events = [(FIRST, -1, 0), (FIRST + 1, -1, 1)]
+    for k in range(1, 2 * nc):
         for h in range(hops + 1):
-            events.append((h if k == 0 else k + h + 1, k, h))
+            events.append((k - 1 + h, k, h))
     events.sort()
     for _, k, h in events:
-        if h == 0 and k < 2 * nc:
+        if k < 0:
+            if h == 0:
+                for d in direct:
+                    z_direct(2, d).wait_recv()
+                build_tables()
+            for d in direct:
+                z_direct(h, d).wait_recv()
+            dispatch(0, h)
+            if h == 1:
+                build_gates()
+            continue
+        if h == 0:
             own_block[k].wait()
         z_step(k, h)
         if h == hops:
-            if k == 2 * nc:
-                build_tables()
-            else:
-                dispatch(k)
-                if k >= LAG:
-                    arrived(k - LAG)
+            dispatch(k)
+            if k >= LAG:
+                arrived(k - LAG)
     back = 0
     for k in range(2 * nc - LAG, 2 * nc):
         if k >= 2 * nc - 2:
@@ -430,49 +489,73 @@
     make_pre_grad()
     weight_grad_up(0)
     y_run((2, 1), (0, 3))
-    send_back(back)
-    back += 1
+    if AHEAD > 2:
+        send_back(back)
+        back += 1
     weight_grad_up(1)
     y_run((3, 1), (1, 2))
     plan = [
-        [(0, 4), (2, 2)],
-        [(1, 3), (3, 2)],
-        [(0, 5), (1, 4)],
-        [(2, 3), (0, 6)],
-        [(1, 5), (2, 4), (3, 3)],
-        [(1, 6), (2, 5), (3, 4)],
-        [(2, 6), (3, 5), (0, 7)],
-        [(3, 6), (1, 7)],
-        [],
-        [(2, 7)],
-        [],
-        [(3, 7)],
+        [(0, 4)],
+        [(1, 3), (2, 2)],
+        [(0, 5), (3, 2)],
+        [(1, 4), (2, 3)],
+        [(0, 6), (3, 3), (1, 5)],
+        [(2, 4), (1, 6), (3, 4)],
+        [(2, 5), (0, 7)],
+        [(3, 5), (2, 6)],
+        [(1, 7), (3, 6)],
+        [(2, 7), (3, 7)],
     ]
-    count = 2 * nc
-    for m in range(count + hops):
-        if back < count:
+
+    def ring_steps(m):
+        for h in range(hops, 0, -1):
+            if 0 <= m - h < ring:
+                s_step(m - h, h)
+
+    for m in range(last):
+        while back <= min(last, m + AHEAD):
             send_back(back)
             back += 1
-        if m < count:
-            combine(m)
-        for h in range(hops, 0, -1):
-            if 0 <= m - h < count:
-                s_step(m - h, h)
-        if m < len(plan):
-            y_run(*plan[m])
-    y_run(*[step for late in plan[count + hops:] for step in late])
-
-    for k in range(2 * nc + 1):
+        ring_steps(m)
+        combine(m)
+        y_run(*plan[m])
+    while back <= last:
+        send_back(back)
+        back += 1
+    ring_steps(last)
+    combine(last, 0)
+    ring_steps(last + 1)
+    y_run(*plan[last])
+    combine(last, 1)
+    for m in range(last + 2, last + hops):
+        ring_steps(m)
+    y_run(*plan[last + 1])
+    for m in range(ring, last):
+        finish(m)
+    finish(last, 0)
+    finish(last, 1)
+    y_run(*plan[last + 2])
+
+    for part in range(3):
+        for d in range(1, nz):
+            z_direct(part, d).wait_send()
+            if part < 2:
+                s_direct(last, part, d).wait_send()
+    for m in range(ring, last):
+        for d in range(1, nz):
+            s_direct(m, None, d).wait_send()
+    for k in range(2 * nc):
+        for j in range(1, nx):
+            for part in (0, 1) if k == 0 else (None,):
+                x_copy(k, j, part).wait_send()
+            for part in (0, 1) if k == last else (None,):
+                c_copy(k, j, part).wait_send()
         for way in (0, 1):
             for h in range(1, ways(k)[way] + 1):
-                z_copy(k, way, h).wait_send()
-    for k in range(2 * nc):
-        for j in range(1, nx):
-            x_copy(k, j).wait_send()
-            c_copy(k, j).wait_send()
-        for way in (0, 1):
-            for h in range(1, ways(k)[way] + 1):
-                s_copy(k, way, h).wait_send()
+                if k > 0:
+                    z_copy(k, way, h).wait_send()
+                if k < ring:
+                    s_copy(k, way, h).wait_send()
     if do_y:
         for w in range(4):
             for name, cp in y_copies(w).items():
@@ -551,14 +634,14 @@
         pltpu.VMEM((2, hid_w // 8, width // 2), BF16),
         pltpu.VMEM((2, width // 16, hid_w), BF16),
         dma((2 + 2 * nc,)),
+        dma((2 * nc + 2, nz - 1)),
+        dma((2 * nc + 2, nz - 1)),
+        dma((2 * nc + 1, nx - 1)),
+        dma((2 * nc + 1, nx - 1)),
+        dma((2 * nc + 1, nx - 1)),
+        dma((2 * nc + 1, nx - 1)),
         dma((2 * nc + 1, nz - 1)),
         dma((2 * nc + 1, nz - 1)),
-        dma((2 * nc, nx - 1)),
-        dma((2 * nc, nx - 1)),
-        dma((2 * nc, nx - 1)),
-        dma((2 * nc, nx - 1)),
-        dma((2 * nc, nz - 1)),
-        dma((2 * nc, nz - 1)),
         dma((4, 15)),
         dma((4, 15)),
         dma((4,)),

time: 164 us -> 159 us (0.970)
  the two profiles are of different devices: /device:TPU:16 before, /device:TPU:1 now
where the time goes in v3:
time: 159 us
  Pallas kernels  158 us (99%)
    pallas_call x1, Pallas kernels, run(): pl.pallas_call(functools.partial(kernel, cfg), out_shape=(jax.ShapeDtypeS...  152 us
    pallas_call x1, Pallas kernels, hand_out(): pl.pallas_call(body, out_shape=tuple((jax.ShapeDtypeStruct(r.shape, r.dty...  5.72 us

profile of v3, /device:TPU:1, one launch (start us, length us, event | category | flops | bytes accessed | tf_op | source)
XLA Modules:
  0.0 158.5 jit_solution(14231698847681453909)
XLA Ops:
  0.6 152.0 %expert_layer.1 = (bf16[48,2048]{1,0:T(8,128)(2,1)}, bf16[48,2048]{1,0:T(8,128)(2,1)}, bf16[1,2048,768]{2,1,0:T(8,128)(2,1)}, bf16[1,768,2048]{2,1,0:T(8,128)(2,1)}) custom-call(bf16[48,2048]{1,0:T(8,128)(2,1)} %refs_0_.1, bf16[48,2048]{1,0:T(8,128)(2,1)} %refs_1_.1, s32[8,48]{1,0:T(8,128)} %bitcast.2, f32[8,48]{1,0:T(8,128)} %bitcast.3, ...), custom_call_target="tpu_custom_call" | custom-call | tf_op jit(solution)/shard_map/expert_layer/pallas_call | solution.py:649
  152.7 5.7 %hand_out.1 = (bf16[48,2048]{1,0:T(8,128)(2,1)}, bf16[48,2048]{1,0:T(8,128)(2,1)}, bf16[1,2048,768]{2,1,0:T(8,128)(2,1)}, bf16[1,768,2048]{2,1,0:T(8,128)(2,1)}) custom-call(bf16[48,2048]{1,0:T(8,128)(2,1)} %get-tuple-element.8.refs_0_, bf16[48,2048]{1,0:T(8,128)(2,1)} %get-tuple-element.9.refs_1_, bf16[1,2048,768]{2,1,0:T(8,128)(2,1)} %get-tuple-element.10.refs_2_, ...), custom_call_target="tpu_custom_call" | custom-call | tf_op jit(solution)/shard_map/hand_out/pallas_call | solution.py:592

commit v4 on v3

--- a/solution.py
+++ b/solution.py
@@ -495,15 +495,15 @@
     weight_grad_up(1)
     y_run((3, 1), (1, 2))
     plan = [
-        [(0, 4)],
-        [(1, 3), (2, 2)],
-        [(0, 5), (3, 2)],
-        [(1, 4), (2, 3)],
-        [(0, 6), (3, 3), (1, 5)],
-        [(2, 4), (1, 6), (3, 4)],
-        [(2, 5), (0, 7)],
-        [(3, 5), (2, 6)],
-        [(1, 7), (3, 6)],
+        [],
+        [(0, 4), (2, 2)],
+        [(1, 3), (3, 2)],
+        [(0, 5), (2, 3)],
+        [(1, 4), (3, 3)],
+        [(0, 6), (2, 4), (1, 5)],
+        [(3, 4), (2, 5)],
+        [(1, 6), (0, 7), (3, 5)],
+        [(2, 6), (1, 7), (3, 6)],
         [(2, 7), (3, 7)],
     ]
 

time: 159 us -> 157 us (0.987)
  Pallas kernels: 158 us -> 156 us
    pallas_call x1, Pallas kernels: 152 us -> 150 us  [run(): pl.pallas_call(functools.partial(kernel, cfg), out_shape=(jax.ShapeDtypeS...]
where the time goes in v4:
time: 157 us
  Pallas kernels  156 us (99%)
    pallas_call x1, Pallas kernels, run(): pl.pallas_call(functools.partial(kernel, cfg), out_shape=(jax.ShapeDtypeS...  150 us
    pallas_call x1, Pallas kernels, hand_out(): pl.pallas_call(body, out_shape=tuple((jax.ShapeDtypeStruct(r.shape, r.dty...  5.72 us

profile of v4, /device:TPU:1, one launch (start us, length us, event | category | flops | bytes accessed | tf_op | source)
XLA Modules:
  0.0 156.6 jit_solution(14457798626393499046)
XLA Ops:
  0.6 150.1 %expert_layer.1 = (bf16[48,2048]{1,0:T(8,128)(2,1)}, bf16[48,2048]{1,0:T(8,128)(2,1)}, bf16[1,2048,768]{2,1,0:T(8,128)(2,1)}, bf16[1,768,2048]{2,1,0:T(8,128)(2,1)}) custom-call(bf16[48,2048]{1,0:T(8,128)(2,1)} %refs_0_.1, bf16[48,2048]{1,0:T(8,128)(2,1)} %refs_1_.1, s32[8,48]{1,0:T(8,128)} %bitcast.2, f32[8,48]{1,0:T(8,128)} %bitcast.3, ...), custom_call_target="tpu_custom_call" | custom-call | tf_op jit(solution)/shard_map/expert_layer/pallas_call | solution.py:649
  150.7 5.7 %hand_out.1 = (bf16[48,2048]{1,0:T(8,128)(2,1)}, bf16[48,2048]{1,0:T(8,128)(2,1)}, bf16[1,2048,768]{2,1,0:T(8,128)(2,1)}, bf16[1,768,2048]{2,1,0:T(8,128)(2,1)}) custom-call(bf16[48,2048]{1,0:T(8,128)(2,1)} %get-tuple-element.8.refs_0_, bf16[48,2048]{1,0:T(8,128)(2,1)} %get-tuple-element.9.refs_1_, bf16[1,2048,768]{2,1,0:T(8,128)(2,1)} %get-tuple-element.10.refs_2_, ...), custom_call_target="tpu_custom_call" | custom-call | tf_op jit(solution)/shard_map/hand_out/pallas_call | solution.py:592
